TPU v7x, 256 devices: a whole 4x4x8 slice. The times are simulated.
256 devices in a mesh: ctx: 32 (over z, y), head: 8 (over x, core).
Axes of the slice: x: 4, y: 4, z: 8, core: 2. Of those that a mesh axis runs over, the one named last changes fastest.
Arguments:
- residual: bfloat16 [8192, 1024], P(('ctx', 'head')), may hold values from -6 to 6
- input_gain: float32 [2, 1024], replicated, may hold values from 0.25 to 1.75
- project_in: bfloat16 [2, 3, 1024, 1024], P(None, None, None, 'head'), may hold values from -0.1875 to 0.1875
- output_gain: float32 [2, 1024], P(None, 'head'), may hold values from 0.25 to 1.75
- project_out: bfloat16 [2, 1024, 1024], P(None, 'head'), may hold values from -0.1875 to 0.1875
Outputs:
- result_rows: bfloat16 [8192, 1024], P(('ctx', 'head'))
All inputs are finite; a program needn't handle non-finite values.
Results may differ from a plain program's by a relative error of at most 0.012.
Values may be sent and summed in bfloat16 or wider, within the bound.
A program may use at most 128 MiB of HBM per device.

v0:
```python
import functools

import jax
import jax.numpy as jnp
from jax import lax
from jax.experimental import pallas as pl
from jax.experimental.pallas import tpu as pltpu
from jax.sharding import PartitionSpec as P

MESH = pl.DeviceIdType.MESH
D = 1024
HD = 64
LAYERS = 2
TOK = 256
NZ = 8
NY = 4
NX = 4
NH = 8
ROWS = TOK // NH
PAIRS = 9
PART = PAIRS * 8
SLICE = NZ * PART
EPS = 1e-06
F32 = jnp.float32
BF16 = jnp.bfloat16
FAR = (1, 3, 2)


def mm(a, b):
    return jnp.dot(a, b, preferred_element_type=F32)


def kernel(
    residual,
    in_gain,
    w_in,
    out_gain,
    w_out,
    result,
    rows_buf,
    win_buf,
    wout_buf,
    kv_buf,
    k_buf,
    q_buf,
    wide_k,
    wide_q,
    feat_k,
    feat_q,
    state,
    state_out,
    state_in,
    prior_out,
    prior_in,
    part_out,
    part_in,
    mix_buf,
    mix_in,
    q_rows,
    inner,
    resid,
    local_sem,
    rows_send,
    rows_recv,
    wout_send,
    wout_recv,
    kv_send,
    kv_recv,
    k_send,
    k_recv,
    q_send,
    q_recv,
    state_send,
    state_recv,
    prior_send,
    prior_recv,
    part_send,
    part_recv,
    mix_send,
    mix_recv,
    last_send,
    last_recv,
):
    ctx = lax.axis_index("ctx")
    head = lax.axis_index("head")
    z, y = ctx // NY, ctx % NY
    x, core = head // 2, head % 2
    sibling = x * 2 + (1 - core)

    def at_x(step):
        return ((x + step) % NX) * 2 + core

    def at_y(step):
        return z * NY + (y + step) % NY

    def at_z(step):
        return ((z + step) % NZ) * NY + y

    def send(src, dst, ssem, rsem, to):
        copy = pltpu.make_async_remote_copy(
            src_ref=src, dst_ref=dst, send_sem=ssem, recv_sem=rsem, device_id=to, device_id_type=MESH
        )
        copy.start()
        return copy

    own_rows = pltpu.make_async_copy(residual, rows_buf.at[head], local_sem.at[0])
    own_rows.start()
    loads = []
    for layer in range(LAYERS):
        for m in range(3):
            load = pltpu.make_async_copy(
                w_in.at[layer, m], win_buf.at[layer, :, pl.ds(m * 128, 128)], local_sem.at[1 + layer * 3 + m]
            )
            load.start()
            loads.append(load)
    own_out = []
    for layer in range(LAYERS):
        load = pltpu.make_async_copy(w_out.at[layer], wout_buf.at[layer, head], local_sem.at[7 + layer])
        load.start()
        own_out.append(load)

    barrier = pltpu.get_barrier_semaphore()
    for step in range(1, NH):
        pl.semaphore_signal(barrier, inc=1, device_id=(ctx, (head + step) % NH), device_id_type=MESH)
    for step in range(1, NY):
        pl.semaphore_signal(barrier, inc=1, device_id=(at_y(step), head), device_id_type=MESH)
    for step in range(1, NZ):
        pl.semaphore_signal(barrier, inc=1, device_id=(at_z(step), head), device_id_type=MESH)
    pl.semaphore_wait(barrier, NH - 1 + NY - 1 + NZ - 1)

    def gather_start(buf, ssem, rsem):
        mine = buf.at[head]
        copies = [send(mine, mine, ssem.at[0], rsem.at[0], (ctx, sibling))]
        for step in FAR:
            copies.append(send(mine, mine, ssem.at[step], rsem.at[step], (ctx, at_x(step))))
        return copies

    def gather_forward(buf, ssem, rsem, copies):
        more = []
        for place, step in enumerate(FAR):
            copies[1 + place].wait_recv()
            got = buf.at[at_x(NX - step)]
            more.append(send(got, got, ssem.at[3 + step], rsem.at[3 + step], (ctx, sibling)))
        return more

    def gather_end(copies, more):
        copies[0].wait_recv()
        for copy in more:
            copy.wait_recv()
        for copy in copies + more:
            copy.wait_send()

    own_rows.wait()
    copies = gather_start(rows_buf, rows_send, rows_recv)
    more = gather_forward(rows_buf, rows_send, rows_recv, copies)
    gather_end(copies, more)
    resid[...] = rows_buf[...].reshape(TOK, D).astype(F32)

    lane = lax.broadcasted_iota(jnp.int32, (1, 128), 1)
    low = lane < HD

    def block_pair(p):
        if p < 8:
            first = 2 * y + p // 4
            return first, (first + p % 4) % 8, (1.0 if p % 4 == 0 else 2.0)
        return y, y + 4, 2.0

    def make_features(wide, feat, slot):
        def head_features(h, carry):
            base = h * HD
            for p in range(PAIRS):
                one, other, _ = block_pair(p)
                block = wide[slot, pl.ds(pl.multiple_of(base + other * 8, 8), 8), :]
                for rr in range(4):
                    pieces = []
                    for o in range(2):
                        row = wide[slot, pl.ds(base + one * 8 + rr * 2 + o, 1), :]
                        pieces.append(block * row)
                    feat[h, pl.ds((rr * PAIRS + p) * 16, 16), pl.ds(slot * TOK, TOK)] = jnp.concatenate(
                        pieces, axis=0
                    ).astype(BF16)
            return carry

        lax.fori_loop(0, 2, head_features, 0)

    for layer in range(LAYERS):
        if layer == 0:
            own_out[0].wait()
            wout_first = gather_start(wout_buf.at[0], wout_send.at[0], wout_recv.at[0])
        wide = resid[...]
        mean_square = jnp.mean(wide * wide, axis=1, keepdims=True)
        normed = (wide * lax.rsqrt(mean_square + EPS) * in_gain[pl.ds(layer, 1), :]).astype(BF16)
        for m in range(3):
            loads[layer * 3 + m].wait()
        fields = mm(normed, win_buf[layer])
        query = fields[:, :128].astype(BF16).astype(F32)
        key = fields[:, 128:256].astype(BF16).astype(F32)
        kv_buf[layer, 0] = fields[:, 256:].astype(BF16)
        key_t = key.T
        k_buf[layer, 0] = key_t.astype(BF16)
        exchange = {}
        for step in FAR:
            to = (at_y(step), head)
            exchange["k", step] = send(
                k_buf.at[layer, 0], k_buf.at[layer, step], k_send.at[layer, step], k_recv.at[layer, step], to
            )
            exchange["v", step] = send(
                kv_buf.at[layer, 0], kv_buf.at[layer, step], kv_send.at[layer, step], kv_recv.at[layer, step], to
            )
        query_t = query.T
        q_buf[layer, 0] = query_t.astype(BF16)
        for step in FAR:
            to = (at_y(step), head)
            exchange["q", step] = send(
                q_buf.at[layer, 0], q_buf.at[layer, step], q_send.at[layer, step], q_recv.at[layer, step], to
            )
        q_rows[pl.ds(0, TOK), :] = jnp.where(low, query, 0.0).astype(BF16)
        q_rows[pl.ds(TOK, TOK), :] = jnp.where(low, 0.0, query).astype(BF16)

        for step in (0,) + FAR:
            if step == 0:
                wide_k[0] = key_t
            else:
                exchange["k", step].wait_recv()
                exchange["v", step].wait_recv()
                wide_k[step] = k_buf[layer, step].astype(F32)
            make_features(wide_k, feat_k, step)
            for h in range(2):
                term = mm(feat_k[h, :, pl.ds(step * TOK, TOK)], kv_buf[layer, step])
                if step == 0:
                    state[h] = term
                else:
                    state[h] += term
        for r in range(NZ):
            pieces = []
            for p in range(PAIRS):
                at = ((r // 2) * PAIRS + p) * 16 + (r % 2) * 8
                both = jnp.where(low, state[0, pl.ds(at, 8), :], state[1, pl.ds(at, 8), :])
                factor = block_pair(p)[2]
                pieces.append(both * factor if factor != 1.0 else both)
            state_out[layer, r] = jnp.concatenate(pieces, axis=0).astype(BF16)
        for step in range(1, NZ):
            exchange["s", step] = send(
                state_out.at[layer, (z + step) % NZ],
                state_in.at[layer, z],
                state_send.at[layer, step],
                state_recv.at[layer, step],
                (at_z(step), head),
            )
        state_in[layer, z] = state_out[layer, z]

        def attend(step):
            scores = mm(q_rows[...], k_buf[layer, step])
            weights = scores * scores
            if step == 0:
                row = lax.broadcasted_iota(jnp.int32, weights.shape, 0) % TOK
                column = lax.broadcasted_iota(jnp.int32, weights.shape, 1)
                weights = jnp.where(row >= column, weights, 0.0)
            return mm(weights.astype(BF16), kv_buf[layer, step])

        inner[...] = attend(0)

        for step in (0,) + FAR:
            if step == 0:
                wide_q[0] = query_t
            else:
                exchange["q", step].wait_recv()
                wide_q[step] = q_buf[layer, step].astype(F32)
            make_features(wide_q, feat_q, step)

        for step in range(1, NZ):
            exchange["s", step].wait_recv()
        running = jnp.zeros((PART, 128), F32)
        for row in range(NZ):
            prior_out[layer, row] = running.astype(BF16)
            if row < NZ - 1:
                running = running + state_in[layer, row].astype(F32)
        for step in range(1, NZ):
            exchange["p", step] = send(
                prior_out.at[layer, (z + step) % NZ],
                prior_in.at[layer, z],
                prior_send.at[layer, step],
                prior_recv.at[layer, step],
                (at_z(step), head),
            )
        prior_in[layer, z] = prior_out[layer, z]

        for step in range(1, NY):

            @pl.when(y >= step)
            def _(step=step):
                inner[...] += attend(step)

        if layer == 0:
            wout_more = gather_forward(wout_buf.at[0], wout_send.at[0], wout_recv.at[0], wout_first)
        else:
            wout_more = gather_forward(wout_buf.at[1], wout_send.at[1], wout_recv.at[1], wout_second)
        inner_t = jnp.where(low, inner[pl.ds(0, TOK), :], inner[pl.ds(TOK, TOK), :]).T

        for step in range(1, NZ):
            exchange["p", step].wait_recv()
        parts = [prior_in[layer, r].astype(F32) for r in range(NZ)]
        pieces = []
        for rr in range(4):
            for p in range(PAIRS):
                for o in range(2):
                    pieces.append(parts[rr * 2 + o][p * 8 : p * 8 + 8])
        prior_t = jnp.concatenate(pieces, axis=0).T.astype(BF16)

        def apply(step):
            return jnp.concatenate(
                [mm(prior_t[h * HD : h * HD + HD], feat_q[h, :, pl.ds(step * TOK, TOK)]) for h in range(2)], axis=0
            )

        for step in FAR:
            part_out[layer, step] = apply(step).astype(BF16)
            exchange["o", step] = send(
                part_out.at[layer, step],
                part_in.at[layer, step],
                part_send.at[layer, step],
                part_recv.at[layer, step],
                (at_y(NY - step), head),
            )
        total = inner_t + apply(0)
        for step in FAR:
            exchange["o", step].wait_recv()
            total += part_in[layer, step].astype(F32)

        scaled = []
        for h in range(2):
            mine = total[h * HD : h * HD + HD]
            mean_square = jnp.mean(mine * mine, axis=0, keepdims=True)
            scaled.append(mine * lax.rsqrt(mean_square + EPS))
        mixed = (jnp.concatenate(scaled, axis=0).T * out_gain[pl.ds(layer, 1), :]).astype(BF16)

        if layer == 0:
            gather_end(wout_first, wout_more)
            mix_buf[head] = mixed
            copies = gather_start(mix_buf, mix_send, mix_recv)
            more = gather_forward(mix_buf, mix_send, mix_recv, copies)
            own_out[1].wait()
            wout_second = gather_start(wout_buf.at[1], wout_send.at[1], wout_recv.at[1])
            gather_end(copies, more)
            columns = jnp.concatenate([mix_buf[n] for n in range(NH)], axis=1)
            delta = mm(columns, wout_buf[0].reshape(D, D))
            resid[...] = (resid[...] + delta).astype(BF16).astype(F32)
        else:
            gather_end(wout_second, wout_more)
            mix_buf[0] = mixed
            copies = []
            for step in range(1, NH):
                to = (head + step) % NH
                copies.append(
                    send(
                        mix_buf.at[0, pl.ds(pl.multiple_of(to * ROWS, ROWS), ROWS)],
                        mix_in.at[head],
                        last_send.at[step],
                        last_recv.at[step],
                        (ctx, to),
                    )
                )
            mine = pl.ds(pl.multiple_of(head * ROWS, ROWS), ROWS)
            mix_in[head] = mix_buf[0, mine]
            for copy in copies:
                copy.wait_recv()
            columns = jnp.concatenate([mix_in[n] for n in range(NH)], axis=1)
            delta = mm(columns, wout_buf[1].reshape(D, D))
            result[...] = (resid[mine, :] + delta).astype(BF16)
            for copy in copies:
                copy.wait_send()
        for copy in exchange.values():
            copy.wait_send()


def per_device(residual, in_gain, w_in, out_gain, w_out):
    any_space = pl.BlockSpec(memory_space=pl.ANY)
    vmem = pl.BlockSpec(memory_space=pltpu.VMEM)
    dma = pltpu.SemaphoreType.DMA
    return pl.pallas_call(
        kernel,
        out_shape=jax.ShapeDtypeStruct((ROWS, D), BF16),
        in_specs=[any_space, vmem, any_space, vmem, any_space],
        out_specs=vmem,
        scratch_shapes=[
            pltpu.VMEM((NH, ROWS, D), BF16),
            pltpu.VMEM((LAYERS, D, 3 * 128), BF16),
            pltpu.VMEM((LAYERS, NH, 128, D), BF16),
            pltpu.VMEM((LAYERS, NY, TOK, 128), BF16),
            pltpu.VMEM((LAYERS, NY, 128, TOK), BF16),
            pltpu.VMEM((LAYERS, NY, 128, TOK), BF16),
            pltpu.VMEM((NY, 128, TOK), F32),
            pltpu.VMEM((NY, 128, TOK), F32),
            pltpu.VMEM((2, SLICE, NY * TOK), BF16),
            pltpu.VMEM((2, SLICE, NY * TOK), BF16),
            pltpu.VMEM((2, SLICE, 128), F32),
            pltpu.VMEM((LAYERS, NZ, PART, 128), BF16),
            pltpu.VMEM((LAYERS, NZ, PART, 128), BF16),
            pltpu.VMEM((LAYERS, NZ, PART, 128), BF16),
            pltpu.VMEM((LAYERS, NZ, PART, 128), BF16),
            pltpu.VMEM((LAYERS, NY, 128, TOK), BF16),
            pltpu.VMEM((LAYERS, NY, 128, TOK), BF16),
            pltpu.VMEM((NH, TOK, 128), BF16),
            pltpu.VMEM((NH, ROWS, 128), BF16),
            pltpu.VMEM((2 * TOK, 128), BF16),
            pltpu.VMEM((2 * TOK, 128), F32),
            pltpu.VMEM((TOK, D), F32),
            dma((9,)),
            dma((7,)),
            dma((7,)),
            dma((LAYERS, 7)),
            dma((LAYERS, 7)),
            dma((LAYERS, NY)),
            dma((LAYERS, NY)),
            dma((LAYERS, NY)),
            dma((LAYERS, NY)),
            dma((LAYERS, NY)),
            dma((LAYERS, NY)),
            dma((LAYERS, NZ)),
            dma((LAYERS, NZ)),
            dma((LAYERS, NZ)),
            dma((LAYERS, NZ)),
            dma((LAYERS, NY)),
            dma((LAYERS, NY)),
            dma((7,)),
            dma((7,)),
            dma((NH,)),
            dma((NH,)),
        ],
        compiler_params=pltpu.CompilerParams(
            collective_id=0, has_side_effects=True, vmem_limit_bytes=48 * 1024 * 1024
        ),
        cost_estimate=pl.CostEstimate(flops=1_500_000_000, bytes_accessed=3_000_000, transcendentals=0),
    )(residual, in_gain, w_in, out_gain, w_out)


def solution(mesh):
    return jax.shard_map(
        per_device,
        mesh=mesh,
        in_specs=(
            P(("ctx", "head"), None),
            P(),
            P(None, None, None, "head"),
            P(None, "head"),
            P(None, "head", None),
        ),
        out_specs=P(("ctx", "head"), None),
        check_vma=False,
    )
```

profile of v0, /device:TPU:1, one launch (start us, length us, event | category | flops | bytes accessed | tf_op | source)
XLA Modules:
  0.0 89.9 jit_solution(4006931681301418273)
XLA Ops:
  0.0 0.0 copy-start
  0.0 1.4 %copy-done = bf16[2,3,1024,128]{3,2,1,0:T(8,128)(2,1)S(1)} copy-done((bf16[2,3,1024,128]{3,2,1,0:T(8,128)(2,1)S(1)}, bf16[2,3,1024,128]{3,2,1,0:T(8,128)(2,1)}, u32[]{:S(2)}) %copy-start) | copy-done | bytes 1572888
  1.4 0.0 copy-start.1
  1.4 1.0 %copy-done.1 = bf16[2,128,1024]{2,1,0:T(8,128)(2,1)S(1)} copy-done((bf16[2,128,1024]{2,1,0:T(8,128)(2,1)S(1)}, bf16[2,128,1024]{2,1,0:T(8,128)(2,1)}, u32[]{:S(2)}) %copy-start.1) | copy-done | bytes 524312
  2.5 0.0 copy-start.2
  2.5 0.8 copy-done.2
  3.3 0.0 copy-start.3
  3.3 0.7 copy-done.3
  4.0 0.0 copy-start.4
  4.0 0.7 copy-done.4
  4.7 84.6 %shard_map.55 = bf16[32,1024]{1,0:T(8,128)(2,1)S(1)} custom-call(bf16[32,1024]{1,0:T(8,128)(2,1)S(1)} %copy-done.2, f32[2,1024]{1,0:T(2,128)S(1)} %copy-done.3, bf16[2,3,1024,128]{3,2,1,0:T(8,128)(2,1)S(1)} %copy-done, f32[2,128]{1,0:T(2,128)S(1)} %copy-done.4, bf16[2,128,1024]{2,1,0:T(8,128)(2,1)S(1)} %copy-done.1), custom_call_target="tpu_custom_call" | custom-call | flops 1500000000 | bytes 3000000 | tf_op jit(solution)/shard_map/pallas_call | solution.py:379
  89.3 0.6 copy.7
Async XLA Ops:
  0.0 1.4 %copy-start = (bf16[2,3,1024,128]{3,2,1,0:T(8,128)(2,1)S(1)}, bf16[2,3,1024,128]{3,2,1,0:T(8,128)(2,1)}, u32[]{:S(2)}) copy-start(bf16[2,3,1024,128]{3,2,1,0:T(8,128)(2,1)} %w_in.1) | copy-start | bytes 4718596
  1.4 1.0 %copy-start.1 = (bf16[2,128,1024]{2,1,0:T(8,128)(2,1)S(1)}, bf16[2,128,1024]{2,1,0:T(8,128)(2,1)}, u32[]{:S(2)}) copy-start(bf16[2,128,1024]{2,1,0:T(8,128)(2,1)} %w_out.1) | copy-start | bytes 1572868
  2.5 0.8 copy-start.2
  3.3 0.7 copy-start.3
  4.0 0.7 copy-start.4
where the time goes:
time: 90.2 us; the launch traced here: 89.9 us
  Pallas kernels  84.6 us (94%)
  local copies, waits for them, and re-layouts  5.29 us (6%)
    pallas_call x1, Pallas kernels, per_device(): pl.pallas_call(kernel, out_shape=jax.ShapeDtypeStruct((ROWS, D), BF16), i...  84.6 us
    unnamed x11, local copies, waits for them, and re-layouts  5.29 us

commit v1 on v0

v1 whole, which is shorter than its diff:
```python
import functools

import jax
import jax.numpy as jnp
from jax import lax
from jax.experimental import pallas as pl
from jax.experimental.pallas import tpu as pltpu
from jax.sharding import PartitionSpec as P

MESH = pl.DeviceIdType.MESH
D = 1024
HD = 64
LAYERS = 2
TOK = 256
NZ = 8
NY = 4
NX = 4
NH = 8
ROWS = TOK // NH
PAIRS = 9
PART = PAIRS * 8
SLICE = NZ * PART
EPS = 1e-06
F32 = jnp.float32
BF16 = jnp.bfloat16
FAR = (1, 3, 2)
ZFAR = (4, 3, 5, 2, 6, 1, 7)
HALF = TOK // 2
HROWS = ROWS // 2


def mm(a, b):
    return jnp.dot(a, b, preferred_element_type=F32)


def kernel(
    residual,
    in_gain_hbm,
    w_in,
    out_gain_hbm,
    w_out,
    result,
    in_gain,
    out_gain,
    rows_buf,
    win_buf,
    wout_buf,
    kv_buf,
    q_buf,
    wide_k,
    wide_q,
    feat_k,
    feat_q,
    state,
    state_out,
    state_in,
    prior_out,
    prior_in,
    part_out,
    part_in,
    mix_buf,
    last_out,
    last_in,
    q_rows,
    inner,
    resid,
    local_sem,
    rows_send,
    rows_recv,
    wout_send,
    wout_recv,
    kv_send,
    kv_recv,
    q_send,
    q_recv,
    state_send,
    state_recv,
    prior_send,
    prior_recv,
    part_send,
    part_recv,
    mix_send,
    mix_recv,
    last_send,
    last_recv,
):
    ctx = lax.axis_index("ctx")
    head = lax.axis_index("head")
    z, y = ctx // NY, ctx % NY
    x, core = head // 2, head % 2
    sibling = x * 2 + (1 - core)

    def at_x(step):
        return ((x + step) % NX) * 2 + core

    def at_y(step):
        return z * NY + (y + step) % NY

    def at_z(step):
        return ((z + step) % NZ) * NY + y

    def send(src, dst, ssem, rsem, to):
        copy = pltpu.make_async_remote_copy(
            src_ref=src, dst_ref=dst, send_sem=ssem, recv_sem=rsem, device_id=to, device_id_type=MESH
        )
        copy.start()
        return copy

    barrier = pltpu.get_barrier_semaphore()
    for step in ZFAR:
        pl.semaphore_signal(barrier, inc=1, device_id=(at_z(step), head), device_id_type=MESH)
    for step in range(1, NY):
        pl.semaphore_signal(barrier, inc=1, device_id=(at_y(step), head), device_id_type=MESH)
    for step in range(1, NH):
        pl.semaphore_signal(barrier, inc=1, device_id=(ctx, (head + step) % NH), device_id_type=MESH)

    def load(src, dst, place):
        copy = pltpu.make_async_copy(src, dst, local_sem.at[place])
        copy.start()
        return copy

    own_rows = [load(residual.at[pl.ds(f * HROWS, HROWS)], rows_buf.at[f, head], f) for f in range(2)]
    gains = [load(in_gain_hbm, in_gain, 2), load(out_gain_hbm, out_gain, 3)]
    loads = [
        [
            load(w_in.at[layer, m], win_buf.at[layer, :, pl.ds(m * 128, 128)], 4 + layer * 3 + m)
            for m in range(3)
        ]
        for layer in range(LAYERS)
    ]
    own_out = [load(w_out.at[layer], wout_buf.at[layer, head], 10 + layer) for layer in range(LAYERS)]

    pl.semaphore_wait(barrier, NH - 1 + NY - 1 + NZ - 1)

    def gather_start(buf, ssem, rsem):
        mine = buf.at[head]
        copies = [send(mine, mine, ssem.at[0], rsem.at[0], (ctx, sibling))]
        for step in FAR:
            copies.append(send(mine, mine, ssem.at[step], rsem.at[step], (ctx, at_x(step))))
        return copies

    def gather_forward(buf, ssem, rsem, copies):
        more = []
        for place, step in enumerate(FAR):
            copies[1 + place].wait_recv()
            got = buf.at[at_x(NX - step)]
            more.append(send(got, got, ssem.at[3 + step], rsem.at[3 + step], (ctx, sibling)))
        return more

    def gather_arrive(copies, more):
        copies[0].wait_recv()
        for copy in more:
            copy.wait_recv()

    lane = lax.broadcasted_iota(jnp.int32, (1, 128), 1)
    low = lane < HD

    def block_pair(p):
        if p < 8:
            first = 2 * y + p // 4
            return first, (first + p % 4) % 8, (1.0 if p % 4 == 0 else 2.0)
        return y, y + 4, 2.0

    def make_features(wide, feat, slot, which):
        def head_features(h, carry):
            base = h * HD
            for f in which:
                for p in range(PAIRS):
                    one, other, _ = block_pair(p)
                    block = wide[slot, f, pl.ds(pl.multiple_of(base + other * 8, 8), 8), :]
                    for rr in range(4):
                        pieces = []
                        for o in range(2):
                            row = wide[slot, f, pl.ds(base + one * 8 + rr * 2 + o, 1), :]
                            pieces.append(block * row)
                        feat[h, pl.ds((rr * PAIRS + p) * 16, 16), pl.ds(slot * TOK + f * HALF, HALF)] = (
                            jnp.concatenate(pieces, axis=0).astype(BF16)
                        )
            return carry

        lax.fori_loop(0, 2, head_features, 0)

    sent = []

    halves = []
    for f in range(2):
        own_rows[f].wait()
        halves.append(gather_start(rows_buf.at[f], rows_send.at[f], rows_recv.at[f]))
    more = [gather_forward(rows_buf.at[f], rows_send.at[f], rows_recv.at[f], halves[f]) for f in range(2)]
    for copy in gains:
        copy.wait()

    for layer in range(LAYERS):
        exchange = {}
        queries = []
        for f in range(2):
            part = pl.ds(f * HALF, HALF)
            gather_arrive(halves[f], more[f])
            sent.extend(halves[f] + more[f])
            if layer == 0:
                wide = rows_buf[f].reshape(HALF, D).astype(F32)
            else:
                columns = jnp.concatenate([mix_buf[f, n] for n in range(NH)], axis=1)
                delta = mm(columns, wout_buf[0].reshape(D, D))
                wide = (resid[part, :] + delta).astype(BF16).astype(F32)
            resid[part, :] = wide
            mean_square = jnp.mean(wide * wide, axis=1, keepdims=True)
            normed = (wide * lax.rsqrt(mean_square + EPS) * in_gain[pl.ds(layer, 1), :]).astype(BF16)
            if f == 0:
                for copy in loads[layer]:
                    copy.wait()
            fields = mm(normed, win_buf[layer])
            key_t = fields[:, 128:256].astype(BF16).astype(F32).T
            kv_buf[layer, 0, 0, f] = key_t.astype(BF16)
            kv_buf[layer, 0, 1, f] = fields[:, 256:].astype(BF16)
            for step in FAR:
                exchange["kv", step, f] = send(
                    kv_buf.at[layer, 0, :, f],
                    kv_buf.at[layer, step, :, f],
                    kv_send.at[layer, step, f],
                    kv_recv.at[layer, step, f],
                    (at_y(step), head),
                )
            query = fields[:, :128].astype(BF16).astype(F32)
            query_t = query.T
            q_buf[layer, 0, f] = query_t.astype(BF16)
            wide_q[0, f] = query_t
            wide_k[0, f] = key_t
            q_rows[part, :] = jnp.where(low, query, 0.0).astype(BF16)
            q_rows[pl.ds(TOK + f * HALF, HALF), :] = jnp.where(low, 0.0, query).astype(BF16)
        for step in FAR:
            exchange["q", step] = send(
                q_buf.at[layer, 0], q_buf.at[layer, step], q_send.at[layer, step], q_recv.at[layer, step], (at_y(step), head)
            )

        own_out[layer].wait()
        wout_copies = gather_start(wout_buf.at[layer], wout_send.at[layer], wout_recv.at[layer])

        def values(step):
            return kv_buf[layer, step, 1].reshape(TOK, 128)

        def add_state(step):
            for h in range(2):
                term = mm(feat_k[h, :, pl.ds(step * TOK, TOK)], values(step))
                if step == 0:
                    state[h] = term
                else:
                    state[h] += term

        make_features(wide_k, feat_k, 0, (0, 1))
        add_state(0)
        for f in range(2):
            for step in FAR:
                exchange["kv", step, f].wait_recv()
                wide_k[step, f] = kv_buf[layer, step, 0, f].astype(F32)
                make_features(wide_k, feat_k, step, (f,))
                if f == 1:
                    add_state(step)
        for r in range(NZ):
            pieces = []
            for p in range(PAIRS):
                at = ((r // 2) * PAIRS + p) * 16 + (r % 2) * 8
                both = jnp.where(low, state[0, pl.ds(at, 8), :], state[1, pl.ds(at, 8), :])
                factor = block_pair(p)[2]
                pieces.append(both * factor if factor != 1.0 else both)
            state_out[layer, r] = jnp.concatenate(pieces, axis=0).astype(BF16)
        for step in ZFAR:
            exchange["s", step] = send(
                state_out.at[layer, (z + step) % NZ],
                state_in.at[layer, z],
                state_send.at[layer, step],
                state_recv.at[layer, step],
                (at_z(step), head),
            )
        state_in[layer, z] = state_out[layer, z]

        def attend(step):
            keys = jnp.concatenate([kv_buf[layer, step, 0, 0], kv_buf[layer, step, 0, 1]], axis=1)
            scores = mm(q_rows[...], keys)
            weights = scores * scores
            if step == 0:
                row = lax.broadcasted_iota(jnp.int32, weights.shape, 0) % TOK
                column = lax.broadcasted_iota(jnp.int32, weights.shape, 1)

                def place(i):
                    return ((i % HALF) // HROWS) * ROWS + (i // HALF) * HROWS + i % HROWS

                weights = jnp.where(place(row) >= place(column), weights, 0.0)
            return mm(weights.astype(BF16), values(step))

        inner[...] = attend(0)

        for step in (0,) + FAR:
            if step != 0:
                exchange["q", step].wait_recv()
                for f in range(2):
                    wide_q[step, f] = q_buf[layer, step, f].astype(F32)
            make_features(wide_q, feat_q, step, (0, 1))

        for step in ZFAR:
            exchange["s", step].wait_recv()
        running = jnp.zeros((PART, 128), F32)
        for row in range(NZ):
            prior_out[layer, row] = running.astype(BF16)
            if row < NZ - 1:
                running = running + state_in[layer, row].astype(F32)
        for step in ZFAR:
            exchange["p", step] = send(
                prior_out.at[layer, (z + step) % NZ],
                prior_in.at[layer, z],
                prior_send.at[layer, step],
                prior_recv.at[layer, step],
                (at_z(step), head),
            )
        prior_in[layer, z] = prior_out[layer, z]

        for step in range(1, NY):

            @pl.when(y >= step)
            def _(step=step):
                inner[...] += attend(step)

        inner_t = jnp.where(low, inner[pl.ds(0, TOK), :], inner[pl.ds(TOK, TOK), :]).T

        for step in ZFAR:
            exchange["p", step].wait_recv()
        parts = [prior_in[layer, r].astype(F32) for r in range(NZ)]
        pieces = []
        for rr in range(4):
            for p in range(PAIRS):
                for o in range(2):
                    pieces.append(parts[rr * 2 + o][p * 8 : p * 8 + 8])
        prior_t = jnp.concatenate(pieces, axis=0).T.astype(BF16)

        def apply(step):
            return jnp.concatenate(
                [mm(prior_t[h * HD : h * HD + HD], feat_q[h, :, pl.ds(step * TOK, TOK)]) for h in range(2)], axis=0
            )

        def give(step, f):
            exchange["o", step, f] = send(
                part_out.at[layer, step, f],
                part_in.at[layer, step, f],
                part_send.at[layer, step, f],
                part_recv.at[layer, step, f],
                (at_y(NY - step), head),
            )

        for step in FAR:
            outer = apply(step).astype(BF16)
            part_out[layer, step, 0] = outer[:, :HALF]
            part_out[layer, step, 1] = outer[:, HALF:]
            give(step, 0)
        for step in FAR:
            give(step, 1)
        wout_more = gather_forward(wout_buf.at[layer], wout_send.at[layer], wout_recv.at[layer], wout_copies)
        sent.extend(wout_copies + wout_more)
        own = inner_t + apply(0)

        if layer == 0:
            gather_arrive(wout_copies, wout_more)
        halves, more = [], []
        for f in range(2):
            total = own[:, f * HALF : f * HALF + HALF]
            for step in FAR:
                exchange["o", step, f].wait_recv()
                total += part_in[layer, step, f].astype(F32)
            scaled = []
            for h in range(2):
                mine = total[h * HD : h * HD + HD]
                mean_square = jnp.mean(mine * mine, axis=0, keepdims=True)
                scaled.append(mine * lax.rsqrt(mean_square + EPS))
            mixed = (jnp.concatenate(scaled, axis=0).T * out_gain[pl.ds(layer, 1), :]).astype(BF16)
            if layer == 0:
                mix_buf[f, head] = mixed
                halves.append(gather_start(mix_buf.at[f], mix_send.at[f], mix_recv.at[f]))
            else:
                last_out[:, f] = mixed.reshape(NH, HROWS, 128)
        if layer == 0:
            more = [gather_forward(mix_buf.at[f], mix_send.at[f], mix_recv.at[f], halves[f]) for f in range(2)]
        else:
            copies = []
            for step in range(1, NH):
                to = (head + step) % NH
                copies.append(
                    send(last_out.at[to], last_in.at[head], last_send.at[step], last_recv.at[step], (ctx, to))
                )
            last_in[head] = last_out[head]
            gather_arrive(wout_copies, wout_more)
            mine = jnp.concatenate(
                [resid[pl.ds(pl.multiple_of(f * HALF + head * HROWS, HROWS), HROWS), :] for f in range(2)], axis=0
            )
            for copy in copies:
                copy.wait_recv()
            columns = jnp.concatenate([last_in[n].reshape(ROWS, 128) for n in range(NH)], axis=1)
            delta = mm(columns, wout_buf[1].reshape(D, D))
            result[...] = (mine + delta).astype(BF16)
            sent.extend(copies)
        sent.extend(exchange.values())
    for copy in sent:
        copy.wait_send()


def per_device(residual, in_gain, w_in, out_gain, w_out):
    hbm = pl.BlockSpec(memory_space=pltpu.HBM)
    vmem = pl.BlockSpec(memory_space=pltpu.VMEM)
    dma = pltpu.SemaphoreType.DMA
    return pl.pallas_call(
        kernel,
        out_shape=jax.ShapeDtypeStruct((ROWS, D), BF16),
        in_specs=[hbm] * 5,
        out_specs=vmem,
        scratch_shapes=[
            pltpu.VMEM((LAYERS, D), F32),
            pltpu.VMEM((LAYERS, 128), F32),
            pltpu.VMEM((2, NH, HROWS, D), BF16),
            pltpu.VMEM((LAYERS, D, 3 * 128), BF16),
            pltpu.VMEM((LAYERS, NH, 128, D), BF16),
            pltpu.VMEM((LAYERS, NY, 2, 2, 128, 128), BF16),
            pltpu.VMEM((LAYERS, NY, 2, 128, HALF), BF16),
            pltpu.VMEM((NY, 2, 128, HALF), F32),
            pltpu.VMEM((NY, 2, 128, HALF), F32),
            pltpu.VMEM((2, SLICE, NY * TOK), BF16),
            pltpu.VMEM((2, SLICE, NY * TOK), BF16),
            pltpu.VMEM((2, SLICE, 128), F32),
            pltpu.VMEM((LAYERS, NZ, PART, 128), BF16),
            pltpu.VMEM((LAYERS, NZ, PART, 128), BF16),
            pltpu.VMEM((LAYERS, NZ, PART, 128), BF16),
            pltpu.VMEM((LAYERS, NZ, PART, 128), BF16),
            pltpu.VMEM((LAYERS, NY, 2, 128, HALF), BF16),
            pltpu.VMEM((LAYERS, NY, 2, 128, HALF), BF16),
            pltpu.VMEM((2, NH, HALF, 128), BF16),
            pltpu.VMEM((NH, 2, HROWS, 128), BF16),
            pltpu.VMEM((NH, 2, HROWS, 128), BF16),
            pltpu.VMEM((2 * TOK, 128), BF16),
            pltpu.VMEM((2 * TOK, 128), F32),
            pltpu.VMEM((TOK, D), F32),
            dma((12,)),
            dma((2, 7)),
            dma((2, 7)),
            dma((LAYERS, 7)),
            dma((LAYERS, 7)),
            dma((LAYERS, NY, 2)),
            dma((LAYERS, NY, 2)),
            dma((LAYERS, NY)),
            dma((LAYERS, NY)),
            dma((LAYERS, NZ)),
            dma((LAYERS, NZ)),
            dma((LAYERS, NZ)),
            dma((LAYERS, NZ)),
            dma((LAYERS, NY, 2)),
            dma((LAYERS, NY, 2)),
            dma((2, 7)),
            dma((2, 7)),
            dma((NH,)),
            dma((NH,)),
        ],
        compiler_params=pltpu.CompilerParams(
            collective_id=0, has_side_effects=True, vmem_limit_bytes=40 * 1024 * 1024
        ),
        cost_estimate=pl.CostEstimate(flops=1_500_000_000, bytes_accessed=3_000_000, transcendentals=0),
    )(*[pltpu.with_memory_space_constraint(a, pltpu.HBM) for a in (residual, in_gain, w_in, out_gain, w_out)])


def solution(mesh):
    return jax.shard_map(
        per_device,
        mesh=mesh,
        in_specs=(
            P(("ctx", "head"), None),
            P(),
            P(None, None, None, "head"),
            P(None, "head"),
            P(None, "head", None),
        ),
        out_specs=P(("ctx", "head"), None),
        check_vma=False,
    )
```

time: 90.2 us -> 78.6 us (0.87)
  Pallas kernels: 84.6 us -> 77.9 us
  local copies, waits for them, and re-layouts: 5.29 us -> 0.63 us
    pallas_call x1, Pallas kernels: 84.6 us -> 77.9 us  [per_device(): pl.pallas_call(kernel, out_shape=jax.ShapeDtypeStruct((ROWS, D), BF16), i...]
    unnamed x11 -> x1, local copies, waits for them, and re-layouts: 5.29 us -> 0.63 us
where the time goes in v1:
time: 78.6 us; the launch traced here: 78.5 us
  Pallas kernels  77.9 us (99%)
    pallas_call x1, Pallas kernels, per_device(): pl.pallas_call(kernel, out_shape=jax.ShapeDtypeStruct((ROWS, D), BF16), i...  77.9 us

profile of v1, /device:TPU:1, one launch (start us, length us, event | category | flops | bytes accessed | tf_op | source)
XLA Modules:
  0.0 78.5 jit_solution(7078298481162266696)
XLA Ops:
  0.0 77.9 %shard_map.55 = bf16[32,1024]{1,0:T(8,128)(2,1)S(1)} custom-call(bf16[32,1024]{1,0:T(8,128)(2,1)} %residual.1, f32[2,1024]{1,0:T(2,128)} %in_gain_hbm.1, bf16[2,3,1024,128]{3,2,1,0:T(8,128)(2,1)} %w_in.1, f32[2,128]{1,0:T(2,128)} %out_gain_hbm.1, bf16[2,128,1024]{2,1,0:T(8,128)(2,1)} %w_out.1), custom_call_target="tpu_custom_call" | custom-call | flops 1500000000 | bytes 3000000 | tf_op jit(solution)/shard_map/pallas_call | solution.py:408
  77.9 0.6 copy.7

commit v2 on v1

--- a/solution.py
+++ b/solution.py
@@ -61,9 +61,12 @@
     mix_buf,
     last_out,
     last_in,
+    normed_buf,
     q_rows,
     inner,
+    attended,
     resid,
+    line_sem,
     local_sem,
     rows_send,
     rows_recv,
@@ -99,16 +102,41 @@
     def at_z(step):
         return ((z + step) % NZ) * NY + y
 
-    def send(src, dst, ssem, rsem, to):
-        copy = pltpu.make_async_remote_copy(
+    def remote(src, dst, ssem, rsem, to):
+        return pltpu.make_async_remote_copy(
             src_ref=src, dst_ref=dst, send_sem=ssem, recv_sem=rsem, device_id=to, device_id_type=MESH
         )
+
+    def send(src, dst, ssem, rsem, to):
+        copy = remote(src, dst, ssem, rsem, to)
         copy.start()
         return copy
 
     barrier = pltpu.get_barrier_semaphore()
-    for step in ZFAR:
-        pl.semaphore_signal(barrier, inc=1, device_id=(at_z(step), head), device_id_type=MESH)
+
+
+    def tell_line(from_above, from_below, reach):
+        @pl.when(z >= reach)
+        def _():
+            pl.semaphore_signal(from_above, inc=1, device_id=(ctx - reach * NY, head), device_id_type=MESH)
+
+        @pl.when(z < NZ - reach)
+        def _():
+            pl.semaphore_signal(from_below, inc=1, device_id=(ctx + reach * NY, head), device_id_type=MESH)
+
+    def tell_round(n):
+        tell_line(line_sem.at[n, 0], line_sem.at[n, 1], 2**n)
+
+    def hear_round(n):
+        @pl.when(z < NZ - 2**n)
+        def _():
+            pl.semaphore_wait(line_sem.at[n, 0], 1)
+
+        @pl.when(z >= 2**n)
+        def _():
+            pl.semaphore_wait(line_sem.at[n, 1], 1)
+
+    tell_line(barrier, barrier, 1)
     for step in range(1, NY):
         pl.semaphore_signal(barrier, inc=1, device_id=(at_y(step), head), device_id_type=MESH)
     for step in range(1, NH):
@@ -130,7 +158,8 @@
     ]
     own_out = [load(w_out.at[layer], wout_buf.at[layer, head], 10 + layer) for layer in range(LAYERS)]
 
-    pl.semaphore_wait(barrier, NH - 1 + NY - 1 + NZ - 1)
+    pl.semaphore_wait(barrier, NH - 1 + NY - 1 + (z + NZ - 1) // NZ + (2 * NZ - 2 - z) // NZ)
+    tell_round(0)
 
     def gather_start(buf, ssem, rsem):
         mine = buf.at[head]
@@ -192,7 +221,6 @@
 
     for layer in range(LAYERS):
         exchange = {}
-        queries = []
         for f in range(2):
             part = pl.ds(f * HALF, HALF)
             gather_arrive(halves[f], more[f])
@@ -209,10 +237,11 @@
             if f == 0:
                 for copy in loads[layer]:
                     copy.wait()
-            fields = mm(normed, win_buf[layer])
-            key_t = fields[:, 128:256].astype(BF16).astype(F32).T
+            normed_buf[part, :] = normed
+            fields = mm(normed, win_buf[layer, :, 128:])
+            key_t = fields[:, :128].astype(BF16).astype(F32).T
             kv_buf[layer, 0, 0, f] = key_t.astype(BF16)
-            kv_buf[layer, 0, 1, f] = fields[:, 256:].astype(BF16)
+            kv_buf[layer, 0, 1, f] = fields[:, 128:].astype(BF16)
             for step in FAR:
                 exchange["kv", step, f] = send(
                     kv_buf.at[layer, 0, :, f],
@@ -221,13 +250,17 @@
                     kv_recv.at[layer, step, f],
                     (at_y(step), head),
                 )
-            query = fields[:, :128].astype(BF16).astype(F32)
-            query_t = query.T
-            q_buf[layer, 0, f] = query_t.astype(BF16)
-            wide_q[0, f] = query_t
             wide_k[0, f] = key_t
-            q_rows[part, :] = jnp.where(low, query, 0.0).astype(BF16)
-            q_rows[pl.ds(TOK + f * HALF, HALF), :] = jnp.where(low, 0.0, query).astype(BF16)
+            if layer == 0 and f == 0:
+                hear_round(0)
+                tell_round(1)
+        query = mm(normed_buf[...], win_buf[layer, :, :128]).astype(BF16).astype(F32)
+        query_t = query.T
+        for f in range(2):
+            wide_q[0, f] = query_t[:, f * HALF : f * HALF + HALF]
+            q_buf[layer, 0, f] = query_t[:, f * HALF : f * HALF + HALF].astype(BF16)
+        q_rows[pl.ds(0, TOK), :] = jnp.where(low, query, 0.0).astype(BF16)
+        q_rows[pl.ds(TOK, TOK), :] = jnp.where(low, 0.0, query).astype(BF16)
         for step in FAR:
             exchange["q", step] = send(
                 q_buf.at[layer, 0], q_buf.at[layer, step], q_send.at[layer, step], q_recv.at[layer, step], (at_y(step), head)
@@ -249,6 +282,9 @@
 
         make_features(wide_k, feat_k, 0, (0, 1))
         add_state(0)
+        if layer == 0:
+            hear_round(1)
+            tell_round(2)
         for f in range(2):
             for step in FAR:
                 exchange["kv", step, f].wait_recv()
@@ -264,6 +300,8 @@
                 factor = block_pair(p)[2]
                 pieces.append(both * factor if factor != 1.0 else both)
             state_out[layer, r] = jnp.concatenate(pieces, axis=0).astype(BF16)
+        if layer == 0:
+            hear_round(2)
         for step in ZFAR:
             exchange["s", step] = send(
                 state_out.at[layer, (z + step) % NZ],
@@ -304,14 +342,22 @@
             prior_out[layer, row] = running.astype(BF16)
             if row < NZ - 1:
                 running = running + state_in[layer, row].astype(F32)
-        for step in ZFAR:
-            exchange["p", step] = send(
+
+        def prior_copy(step):
+            return remote(
                 prior_out.at[layer, (z + step) % NZ],
                 prior_in.at[layer, z],
                 prior_send.at[layer, step],
                 prior_recv.at[layer, step],
                 (at_z(step), head),
             )
+
+        for step in ZFAR:
+
+            @pl.when((z + step) % NZ != 0)
+            def _(step=step):
+                prior_copy(step).start()
+
         prior_in[layer, z] = prior_out[layer, z]
 
         for step in range(1, NY):
@@ -320,25 +366,10 @@
             def _(step=step):
                 inner[...] += attend(step)
 
-        inner_t = jnp.where(low, inner[pl.ds(0, TOK), :], inner[pl.ds(TOK, TOK), :]).T
-
-        for step in ZFAR:
-            exchange["p", step].wait_recv()
-        parts = [prior_in[layer, r].astype(F32) for r in range(NZ)]
-        pieces = []
-        for rr in range(4):
-            for p in range(PAIRS):
-                for o in range(2):
-                    pieces.append(parts[rr * 2 + o][p * 8 : p * 8 + 8])
-        prior_t = jnp.concatenate(pieces, axis=0).T.astype(BF16)
-
-        def apply(step):
-            return jnp.concatenate(
-                [mm(prior_t[h * HD : h * HD + HD], feat_q[h, :, pl.ds(step * TOK, TOK)]) for h in range(2)], axis=0
-            )
-
-        def give(step, f):
-            exchange["o", step, f] = send(
+        attended[...] = jnp.where(low, inner[pl.ds(0, TOK), :], inner[pl.ds(TOK, TOK), :]).T
+
+        def part_copy(step, f):
+            return remote(
                 part_out.at[layer, step, f],
                 part_in.at[layer, step, f],
                 part_send.at[layer, step, f],
@@ -346,25 +377,47 @@
                 (at_y(NY - step), head),
             )
 
-        for step in FAR:
-            outer = apply(step).astype(BF16)
-            part_out[layer, step, 0] = outer[:, :HALF]
-            part_out[layer, step, 1] = outer[:, HALF:]
-            give(step, 0)
-        for step in FAR:
-            give(step, 1)
+        @pl.when(z > 0)
+        def _():
+            for step in ZFAR:
+                prior_copy(step).wait_recv()
+            parts = [prior_in[layer, r].astype(F32) for r in range(NZ)]
+            pieces = []
+            for rr in range(4):
+                for p in range(PAIRS):
+                    for o in range(2):
+                        pieces.append(parts[rr * 2 + o][p * 8 : p * 8 + 8])
+            prior_t = jnp.concatenate(pieces, axis=0).T.astype(BF16)
+
+            def apply(step):
+                return jnp.concatenate(
+                    [mm(prior_t[h * HD : h * HD + HD], feat_q[h, :, pl.ds(step * TOK, TOK)]) for h in range(2)], axis=0
+                )
+
+            for step in FAR:
+                outer = apply(step).astype(BF16)
+                part_out[layer, step, 0] = outer[:, :HALF]
+                part_out[layer, step, 1] = outer[:, HALF:]
+                part_copy(step, 0).start()
+            for step in FAR:
+                part_copy(step, 1).start()
+            attended[...] += apply(0)
+
         wout_more = gather_forward(wout_buf.at[layer], wout_send.at[layer], wout_recv.at[layer], wout_copies)
         sent.extend(wout_copies + wout_more)
-        own = inner_t + apply(0)
-
         if layer == 0:
             gather_arrive(wout_copies, wout_more)
         halves, more = [], []
         for f in range(2):
-            total = own[:, f * HALF : f * HALF + HALF]
-            for step in FAR:
-                exchange["o", step, f].wait_recv()
-                total += part_in[layer, step, f].astype(F32)
+            part = pl.ds(f * HALF, HALF)
+
+            @pl.when(z > 0)
+            def _(f=f, part=part):
+                for step in FAR:
+                    part_copy(step, f).wait_recv()
+                attended[:, part] += sum(part_in[layer, step, f].astype(F32) for step in FAR)
+
+            total = attended[:, part]
             scaled = []
             for h in range(2):
                 mine = total[h * HD : h * HD + HD]
@@ -397,6 +450,18 @@
             result[...] = (mine + delta).astype(BF16)
             sent.extend(copies)
         sent.extend(exchange.values())
+        for step in ZFAR:
+
+            @pl.when((z + step) % NZ != 0)
+            def _(step=step):
+                prior_copy(step).wait_send()
+
+        @pl.when(z > 0)
+        def _():
+            for f in range(2):
+                for step in FAR:
+                    part_copy(step, f).wait_send()
+
     for copy in sent:
         copy.wait_send()
 
@@ -432,9 +497,12 @@
             pltpu.VMEM((2, NH, HALF, 128), BF16),
             pltpu.VMEM((NH, 2, HROWS, 128), BF16),
             pltpu.VMEM((NH, 2, HROWS, 128), BF16),
+            pltpu.VMEM((TOK, D), BF16),
             pltpu.VMEM((2 * TOK, 128), BF16),
             pltpu.VMEM((2 * TOK, 128), F32),
+            pltpu.VMEM((128, TOK), F32),
             pltpu.VMEM((TOK, D), F32),
+            pltpu.SemaphoreType.REGULAR((3, 2)),
             dma((12,)),
             dma((2, 7)),
             dma((2, 7)),

time: 78.6 us -> 75.8 us (0.964)
  the two profiles are of different devices: /device:TPU:1 before, /device:TPU:65 now
where the time goes in v2:
time: 75.8 us; the launch traced here: 75 us
  Pallas kernels  74.4 us (98%)
    pallas_call x1, Pallas kernels, per_device(): pl.pallas_call(kernel, out_shape=jax.ShapeDtypeStruct((ROWS, D), BF16), i...  74.4 us

profile of v2, /device:TPU:65, one launch (start us, length us, event | category | flops | bytes accessed | tf_op | source)
XLA Modules:
  0.0 75.0 jit_solution(15545797371424706961)
XLA Ops:
  0.0 74.4 %shard_map.55 = bf16[32,1024]{1,0:T(8,128)(2,1)S(1)} custom-call(bf16[32,1024]{1,0:T(8,128)(2,1)} %residual.1, f32[2,1024]{1,0:T(2,128)} %in_gain_hbm.1, bf16[2,3,1024,128]{3,2,1,0:T(8,128)(2,1)} %w_in.1, f32[2,128]{1,0:T(2,128)} %out_gain_hbm.1, bf16[2,128,1024]{2,1,0:T(8,128)(2,1)} %w_out.1), custom_call_target="tpu_custom_call" | custom-call | flops 1500000000 | bytes 3000000 | tf_op jit(solution)/shard_map/pallas_call | solution.py:473
  74.4 0.6 copy.7

commit v3 on v2

--- a/solution.py
+++ b/solution.py
@@ -33,6 +33,10 @@
     return jnp.dot(a, b, preferred_element_type=F32)
 
 
+def mm_t(a, b):
+    return lax.dot_general(a, b, (((1,), (1,)), ((), ())), preferred_element_type=F32)
+
+
 def kernel(
     residual,
     in_gain_hbm,
@@ -45,8 +49,10 @@
     rows_buf,
     win_buf,
     wout_buf,
-    kv_buf,
-    q_buf,
+    kv_out,
+    kv_in,
+    q_out,
+    q_in,
     wide_k,
     wide_q,
     feat_k,
@@ -64,7 +70,7 @@
     normed_buf,
     q_rows,
     inner,
-    attended,
+    acc,
     resid,
     line_sem,
     local_sem,
@@ -91,6 +97,7 @@
     head = lax.axis_index("head")
     z, y = ctx // NY, ctx % NY
     x, core = head // 2, head % 2
+    mine, half = y % 2, y // 2
     sibling = x * 2 + (1 - core)
 
     def at_x(step):
@@ -184,30 +191,31 @@
     lane = lax.broadcasted_iota(jnp.int32, (1, 128), 1)
     low = lane < HD
 
-    def block_pair(p):
-        if p < 8:
-            first = 2 * y + p // 4
-            return first, (first + p % 4) % 8, (1.0 if p % 4 == 0 else 2.0)
-        return y, y + 4, 2.0
+    def factor(p):
+        return 1.0 if p < 8 and p % 4 == 0 else 2.0
 
     def make_features(wide, feat, slot, which):
-        def head_features(h, carry):
-            base = h * HD
+        def quarter_features(g, carry):
+            quarter = 2 * half + g
             for f in which:
                 for p in range(PAIRS):
-                    one, other, _ = block_pair(p)
-                    block = wide[slot, f, pl.ds(pl.multiple_of(base + other * 8, 8), 8), :]
+                    if p < 8:
+                        one = 2 * quarter + p // 4
+                        other = (one + p % 4) % 8
+                    else:
+                        one, other = quarter, quarter + 4
+                    block = wide[slot, f, pl.ds(pl.multiple_of(other * 8, 8), 8), :]
                     for rr in range(4):
                         pieces = []
                         for o in range(2):
-                            row = wide[slot, f, pl.ds(base + one * 8 + rr * 2 + o, 1), :]
+                            row = wide[slot, f, pl.ds(one * 8 + rr * 2 + o, 1), :]
                             pieces.append(block * row)
-                        feat[h, pl.ds((rr * PAIRS + p) * 16, 16), pl.ds(slot * TOK + f * HALF, HALF)] = (
+                        feat[g, pl.ds((rr * PAIRS + p) * 16, 16), pl.ds(slot * TOK + f * HALF, HALF)] = (
                             jnp.concatenate(pieces, axis=0).astype(BF16)
                         )
             return carry
 
-        lax.fori_loop(0, 2, head_features, 0)
+        lax.fori_loop(0, 2, quarter_features, 0)
 
     sent = []
 
@@ -239,46 +247,57 @@
                     copy.wait()
             normed_buf[part, :] = normed
             fields = mm(normed, win_buf[layer, :, 128:])
-            key_t = fields[:, :128].astype(BF16).astype(F32).T
-            kv_buf[layer, 0, 0, f] = key_t.astype(BF16)
-            kv_buf[layer, 0, 1, f] = fields[:, 128:].astype(BF16)
+            fields_t = fields.astype(BF16).astype(F32).T
+            for h in range(2):
+                kv_out[layer, h, f] = jnp.concatenate(
+                    [fields_t[h * HD : h * HD + HD], fields_t[128 + h * HD : 128 + h * HD + HD]], axis=0
+                ).astype(BF16)
             for step in FAR:
                 exchange["kv", step, f] = send(
-                    kv_buf.at[layer, 0, :, f],
-                    kv_buf.at[layer, step, :, f],
+                    kv_out.at[layer, (y + step) % 2, f],
+                    kv_in.at[layer, step, f],
                     kv_send.at[layer, step, f],
                     kv_recv.at[layer, step, f],
                     (at_y(step), head),
                 )
-            wide_k[0, f] = key_t
+            own_kv = kv_out[layer, mine, f]
+            kv_in[layer, 0, f] = own_kv
+            wide_k[0, f] = own_kv[:HD].astype(F32)
             if layer == 0 and f == 0:
                 hear_round(0)
                 tell_round(1)
         query = mm(normed_buf[...], win_buf[layer, :, :128]).astype(BF16).astype(F32)
         query_t = query.T
-        for f in range(2):
-            wide_q[0, f] = query_t[:, f * HALF : f * HALF + HALF]
-            q_buf[layer, 0, f] = query_t[:, f * HALF : f * HALF + HALF].astype(BF16)
-        q_rows[pl.ds(0, TOK), :] = jnp.where(low, query, 0.0).astype(BF16)
-        q_rows[pl.ds(TOK, TOK), :] = jnp.where(low, 0.0, query).astype(BF16)
+        for h in range(2):
+            for f in range(2):
+                q_out[layer, h, f] = query_t[h * HD : h * HD + HD, f * HALF : f * HALF + HALF].astype(BF16)
         for step in FAR:
             exchange["q", step] = send(
-                q_buf.at[layer, 0], q_buf.at[layer, step], q_send.at[layer, step], q_recv.at[layer, step], (at_y(step), head)
+                q_out.at[layer, (y + step) % 2],
+                q_in.at[layer, step],
+                q_send.at[layer, step],
+                q_recv.at[layer, step],
+                (at_y(step), head),
             )
-
+        q_in[layer, 0] = q_out[layer, mine]
         own_out[layer].wait()
         wout_copies = gather_start(wout_buf.at[layer], wout_send.at[layer], wout_recv.at[layer])
 
+        def keys(step):
+            return jnp.concatenate([kv_in[layer, step, f, :HD] for f in range(2)], axis=1)
+
         def values(step):
-            return kv_buf[layer, step, 1].reshape(TOK, 128)
+            return jnp.concatenate([kv_in[layer, step, f, HD:] for f in range(2)], axis=1)
 
         def add_state(step):
-            for h in range(2):
-                term = mm(feat_k[h, :, pl.ds(step * TOK, TOK)], values(step))
+            value = values(step)
+            twice = jnp.concatenate([value, value], axis=0)
+            for g in range(2):
+                term = mm_t(feat_k[g, :, pl.ds(step * TOK, TOK)], twice)
                 if step == 0:
-                    state[h] = term
+                    state[g] = term
                 else:
-                    state[h] += term
+                    state[g] += term
 
         make_features(wide_k, feat_k, 0, (0, 1))
         add_state(0)
@@ -288,7 +307,7 @@
         for f in range(2):
             for step in FAR:
                 exchange["kv", step, f].wait_recv()
-                wide_k[step, f] = kv_buf[layer, step, 0, f].astype(F32)
+                wide_k[step, f] = kv_in[layer, step, f, :HD].astype(F32)
                 make_features(wide_k, feat_k, step, (f,))
                 if f == 1:
                     add_state(step)
@@ -297,8 +316,7 @@
             for p in range(PAIRS):
                 at = ((r // 2) * PAIRS + p) * 16 + (r % 2) * 8
                 both = jnp.where(low, state[0, pl.ds(at, 8), :], state[1, pl.ds(at, 8), :])
-                factor = block_pair(p)[2]
-                pieces.append(both * factor if factor != 1.0 else both)
+                pieces.append(both * factor(p))
             state_out[layer, r] = jnp.concatenate(pieces, axis=0).astype(BF16)
         if layer == 0:
             hear_round(2)
@@ -312,28 +330,28 @@
             )
         state_in[layer, z] = state_out[layer, z]
 
-        def attend(step):
-            keys = jnp.concatenate([kv_buf[layer, step, 0, 0], kv_buf[layer, step, 0, 1]], axis=1)
-            scores = mm(q_rows[...], keys)
-            weights = scores * scores
-            if step == 0:
-                row = lax.broadcasted_iota(jnp.int32, weights.shape, 0) % TOK
-                column = lax.broadcasted_iota(jnp.int32, weights.shape, 1)
-
-                def place(i):
-                    return ((i % HALF) // HROWS) * ROWS + (i // HALF) * HROWS + i % HROWS
-
-                weights = jnp.where(place(row) >= place(column), weights, 0.0)
-            return mm(weights.astype(BF16), values(step))
-
-        inner[...] = attend(0)
-
         for step in (0,) + FAR:
             if step != 0:
                 exchange["q", step].wait_recv()
-                for f in range(2):
-                    wide_q[step, f] = q_buf[layer, step, f].astype(F32)
+            for f in range(2):
+                wide_q[step, f] = q_in[layer, step, f].astype(F32)
             make_features(wide_q, feat_q, step, (0, 1))
+            q_rows[pl.ds(step * HALF, HALF), :] = wide_q[step, half].T.astype(BF16)
+
+        def token(shard, i):
+            return shard * TOK + ((i % HALF) // HROWS) * ROWS + (i // HALF) * HROWS + i % HROWS
+
+        row = lax.broadcasted_iota(jnp.int32, (2 * TOK, 1), 0)
+        row_token = token((y + NY - row // HALF) % NY, half * HALF + row % HALF)
+        column = lax.broadcasted_iota(jnp.int32, (1, TOK), 1)
+
+        def attend(step):
+            scores = mm(q_rows[...], keys(step))
+            column_token = token((y + NY - step) % NY, column)
+            weights = jnp.where(row_token >= column_token, scores * scores, 0.0)
+            return mm_t(weights.astype(BF16), values(step))
+
+        inner[...] = attend(0)
 
         for step in ZFAR:
             exchange["s", step].wait_recv()
@@ -361,12 +379,10 @@
         prior_in[layer, z] = prior_out[layer, z]
 
         for step in range(1, NY):
-
-            @pl.when(y >= step)
-            def _(step=step):
-                inner[...] += attend(step)
-
-        attended[...] = jnp.where(low, inner[pl.ds(0, TOK), :], inner[pl.ds(TOK, TOK), :]).T
+            inner[...] += attend(step)
+        for step in range(NY):
+            acc[step, half] = inner[pl.ds(step * HALF, HALF), :].T
+            acc[step, 1 - half] = jnp.zeros((HD, HALF), F32)
 
         def part_copy(step, f):
             return remote(
@@ -390,18 +406,26 @@
             prior_t = jnp.concatenate(pieces, axis=0).T.astype(BF16)
 
             def apply(step):
-                return jnp.concatenate(
-                    [mm(prior_t[h * HD : h * HD + HD], feat_q[h, :, pl.ds(step * TOK, TOK)]) for h in range(2)], axis=0
-                )
+                columns = pl.ds(step * TOK, TOK)
+                return mm(prior_t[:HD], feat_q[0, :, columns]) + mm(prior_t[HD:], feat_q[1, :, columns])
 
             for step in FAR:
-                outer = apply(step).astype(BF16)
-                part_out[layer, step, 0] = outer[:, :HALF]
-                part_out[layer, step, 1] = outer[:, HALF:]
+                outer = apply(step)
+                for f in range(2):
+                    part_out[layer, step, f] = (acc[step, f] + outer[:, f * HALF : f * HALF + HALF]).astype(BF16)
                 part_copy(step, 0).start()
             for step in FAR:
                 part_copy(step, 1).start()
-            attended[...] += apply(0)
+            outer = apply(0)
+            for f in range(2):
+                acc[0, f] += outer[:, f * HALF : f * HALF + HALF]
+
+        @pl.when(z == 0)
+        def _():
+            for f in range(2):
+                for step in FAR:
+                    part_out[layer, step, f] = acc[step, f].astype(BF16)
+                    part_copy(step, f).start()
 
         wout_more = gather_forward(wout_buf.at[layer], wout_send.at[layer], wout_recv.at[layer], wout_copies)
         sent.extend(wout_copies + wout_more)
@@ -409,20 +433,16 @@
             gather_arrive(wout_copies, wout_more)
         halves, more = [], []
         for f in range(2):
-            part = pl.ds(f * HALF, HALF)
-
-            @pl.when(z > 0)
-            def _(f=f, part=part):
-                for step in FAR:
-                    part_copy(step, f).wait_recv()
-                attended[:, part] += sum(part_in[layer, step, f].astype(F32) for step in FAR)
-
-            total = attended[:, part]
+            for step in FAR:
+                part_copy(step, f).wait_recv()
             scaled = []
-            for h in range(2):
-                mine = total[h * HD : h * HD + HD]
-                mean_square = jnp.mean(mine * mine, axis=0, keepdims=True)
-                scaled.append(mine * lax.rsqrt(mean_square + EPS))
+            for total in (
+                acc[0, f] + part_in[layer, 2, f].astype(F32),
+                part_in[layer, 1, f].astype(F32) + part_in[layer, 3, f].astype(F32),
+            ):
+                mean_square = jnp.mean(total * total, axis=0, keepdims=True)
+                scaled.append(total * lax.rsqrt(mean_square + EPS))
+            scaled = [jnp.where(mine == 0, scaled[0], scaled[1]), jnp.where(mine == 0, scaled[1], scaled[0])]
             mixed = (jnp.concatenate(scaled, axis=0).T * out_gain[pl.ds(layer, 1), :]).astype(BF16)
             if layer == 0:
                 mix_buf[f, head] = mixed
@@ -440,14 +460,14 @@
                 )
             last_in[head] = last_out[head]
             gather_arrive(wout_copies, wout_more)
-            mine = jnp.concatenate(
+            before = jnp.concatenate(
                 [resid[pl.ds(pl.multiple_of(f * HALF + head * HROWS, HROWS), HROWS), :] for f in range(2)], axis=0
             )
             for copy in copies:
                 copy.wait_recv()
             columns = jnp.concatenate([last_in[n].reshape(ROWS, 128) for n in range(NH)], axis=1)
             delta = mm(columns, wout_buf[1].reshape(D, D))
-            result[...] = (mine + delta).astype(BF16)
+            result[...] = (before + delta).astype(BF16)
             sent.extend(copies)
         sent.extend(exchange.values())
         for step in ZFAR:
@@ -456,11 +476,9 @@
             def _(step=step):
                 prior_copy(step).wait_send()
 
-        @pl.when(z > 0)
-        def _():
-            for f in range(2):
-                for step in FAR:
-                    part_copy(step, f).wait_send()
+        for f in range(2):
+            for step in FAR:
+                part_copy(step, f).wait_send()
 
     for copy in sent:
         copy.wait_send()
@@ -481,10 +499,12 @@
             pltpu.VMEM((2, NH, HROWS, D), BF16),
             pltpu.VMEM((LAYERS, D, 3 * 128), BF16),
             pltpu.VMEM((LAYERS, NH, 128, D), BF16),
-            pltpu.VMEM((LAYERS, NY, 2, 2, 128, 128), BF16),
+            pltpu.VMEM((LAYERS, 2, 2, 128, HALF), BF16),
             pltpu.VMEM((LAYERS, NY, 2, 128, HALF), BF16),
-            pltpu.VMEM((NY, 2, 128, HALF), F32),
-            pltpu.VMEM((NY, 2, 128, HALF), F32),
+            pltpu.VMEM((LAYERS, 2, 2, HD, HALF), BF16),
+            pltpu.VMEM((LAYERS, NY, 2, HD, HALF), BF16),
+            pltpu.VMEM((NY, 2, HD, HALF), F32),
+            pltpu.VMEM((NY, 2, HD, HALF), F32),
             pltpu.VMEM((2, SLICE, NY * TOK), BF16),
             pltpu.VMEM((2, SLICE, NY * TOK), BF16),
             pltpu.VMEM((2, SLICE, 128), F32),
@@ -492,15 +512,15 @@
             pltpu.VMEM((LAYERS, NZ, PART, 128), BF16),
             pltpu.VMEM((LAYERS, NZ, PART, 128), BF16),
             pltpu.VMEM((LAYERS, NZ, PART, 128), BF16),
-            pltpu.VMEM((LAYERS, NY, 2, 128, HALF), BF16),
-            pltpu.VMEM((LAYERS, NY, 2, 128, HALF), BF16),
+            pltpu.VMEM((LAYERS, NY, 2, HD, HALF), BF16),
+            pltpu.VMEM((LAYERS, NY, 2, HD, HALF), BF16),
             pltpu.VMEM((2, NH, HALF, 128), BF16),
             pltpu.VMEM((NH, 2, HROWS, 128), BF16),
             pltpu.VMEM((NH, 2, HROWS, 128), BF16),
             pltpu.VMEM((TOK, D), BF16),
-            pltpu.VMEM((2 * TOK, 128), BF16),
-            pltpu.VMEM((2 * TOK, 128), F32),
-            pltpu.VMEM((128, TOK), F32),
+            pltpu.VMEM((2 * TOK, HD), BF16),
+            pltpu.VMEM((2 * TOK, HD), F32),
+            pltpu.VMEM((NY, 2, HD, HALF), F32),
             pltpu.VMEM((TOK, D), F32),
             pltpu.SemaphoreType.REGULAR((3, 2)),
             dma((12,)),

time: 75.8 us -> 69.9 us (0.922)
  Pallas kernels: 74.4 us -> 68.4 us
    pallas_call x1, Pallas kernels: 74.4 us -> 68.4 us  [per_device(): pl.pallas_call(kernel, out_shape=jax.ShapeDtypeStruct((ROWS, D), BF16), i...]
where the time goes in v3:
time: 69.9 us; the launch traced here: 69.1 us
  Pallas kernels  68.4 us (98%)
    pallas_call x1, Pallas kernels, per_device(): pl.pallas_call(kernel, out_shape=jax.ShapeDtypeStruct((ROWS, D), BF16), i...  68.4 us

profile of v3, /device:TPU:65, one launch (start us, length us, event | category | flops | bytes accessed | tf_op | source)
XLA Modules:
  0.0 69.1 jit_solution(10416658833235707451)
XLA Ops:
  0.0 68.4 %shard_map.55 = bf16[32,1024]{1,0:T(8,128)(2,1)S(1)} custom-call(bf16[32,1024]{1,0:T(8,128)(2,1)} %residual.1, f32[2,1024]{1,0:T(2,128)} %in_gain_hbm.1, bf16[2,3,1024,128]{3,2,1,0:T(8,128)(2,1)} %w_in.1, f32[2,128]{1,0:T(2,128)} %out_gain_hbm.1, bf16[2,128,1024]{2,1,0:T(8,128)(2,1)} %w_out.1), custom_call_target="tpu_custom_call" | custom-call | flops 1500000000 | bytes 3000000 | tf_op jit(solution)/shard_map/pallas_call | solution.py:491
  68.4 0.6 copy.7

commit v4 on v3

--- a/solution.py
+++ b/solution.py
@@ -24,6 +24,7 @@
 F32 = jnp.float32
 BF16 = jnp.bfloat16
 FAR = (1, 3, 2)
+NEAR = 2
 ZFAR = (4, 3, 5, 2, 6, 1, 7)
 HALF = TOK // 2
 HROWS = ROWS // 2
@@ -62,6 +63,7 @@
     state_in,
     prior_out,
     prior_in,
+    early_in,
     part_out,
     part_in,
     mix_buf,
@@ -86,6 +88,8 @@
     state_recv,
     prior_send,
     prior_recv,
+    early_send,
+    early_recv,
     part_send,
     part_recv,
     mix_send,
@@ -311,24 +315,41 @@
                 make_features(wide_k, feat_k, step, (f,))
                 if f == 1:
                     add_state(step)
-        for r in range(NZ):
+        if layer == 0:
+            hear_round(2)
+        for step in ZFAR + (0,):
+            r = (z + step) % NZ
+            first = (r // 2) * (PAIRS * 16) + (r % 2) * 8
             pieces = []
             for p in range(PAIRS):
-                at = ((r // 2) * PAIRS + p) * 16 + (r % 2) * 8
-                both = jnp.where(low, state[0, pl.ds(at, 8), :], state[1, pl.ds(at, 8), :])
-                pieces.append(both * factor(p))
+                rows = pl.ds(pl.multiple_of(first + p * 16, 8), 8)
+                pieces.append(jnp.where(low, state[0, rows, :], state[1, rows, :]) * factor(p))
             state_out[layer, r] = jnp.concatenate(pieces, axis=0).astype(BF16)
-        if layer == 0:
-            hear_round(2)
-        for step in ZFAR:
-            exchange["s", step] = send(
-                state_out.at[layer, (z + step) % NZ],
-                state_in.at[layer, z],
-                state_send.at[layer, step],
-                state_recv.at[layer, step],
-                (at_z(step), head),
+            if step:
+                exchange["s", step] = send(
+                    state_out.at[layer, r],
+                    state_in.at[layer, z],
+                    state_send.at[layer, step],
+                    state_recv.at[layer, step],
+                    (at_z(step), head),
+                )
+        state_in[layer, z] = state_out[layer, z]
+
+        def early_copy(reach):
+            return remote(
+                state_out.at[layer],
+                early_in.at[layer, reach - 1],
+                early_send.at[layer, reach - 1],
+                early_recv.at[layer, reach - 1],
+                (ctx + reach * NY, head),
             )
-        state_in[layer, z] = state_out[layer, z]
+
+        for reach in range(1, NEAR):
+
+            @pl.when(z < NEAR - reach)
+            def _(reach=reach):
+                early_copy(reach).start()
+
 
         for step in (0,) + FAR:
             if step != 0:
@@ -372,7 +393,7 @@
 
         for step in ZFAR:
 
-            @pl.when((z + step) % NZ != 0)
+            @pl.when((z + step) % NZ >= NEAR)
             def _(step=step):
                 prior_copy(step).start()
 
@@ -395,8 +416,23 @@
 
         @pl.when(z > 0)
         def _():
-            for step in ZFAR:
-                prior_copy(step).wait_recv()
+            @pl.when(z >= NEAR)
+            def _():
+                for step in ZFAR:
+                    prior_copy(step).wait_recv()
+
+            @pl.when(z < NEAR)
+            def _():
+                early_copy(1).wait_recv()
+                prior_in[layer] = early_in[layer, 0]
+
+            for reach in range(2, NEAR):
+
+                @pl.when((z < NEAR) & (z >= reach))
+                def _(reach=reach):
+                    early_copy(reach).wait_recv()
+                    prior_in[layer] = (prior_in[layer].astype(F32) + early_in[layer, reach - 1].astype(F32)).astype(BF16)
+
             parts = [prior_in[layer, r].astype(F32) for r in range(NZ)]
             pieces = []
             for rr in range(4):
@@ -472,9 +508,15 @@
         sent.extend(exchange.values())
         for step in ZFAR:
 
-            @pl.when((z + step) % NZ != 0)
+            @pl.when((z + step) % NZ >= NEAR)
             def _(step=step):
                 prior_copy(step).wait_send()
+
+        for reach in range(1, NEAR):
+
+            @pl.when(z < NEAR - reach)
+            def _(reach=reach):
+                early_copy(reach).wait_send()
 
         for f in range(2):
             for step in FAR:
@@ -512,6 +554,7 @@
             pltpu.VMEM((LAYERS, NZ, PART, 128), BF16),
             pltpu.VMEM((LAYERS, NZ, PART, 128), BF16),
             pltpu.VMEM((LAYERS, NZ, PART, 128), BF16),
+            pltpu.VMEM((LAYERS, NEAR - 1, NZ, PART, 128), BF16),
             pltpu.VMEM((LAYERS, NY, 2, HD, HALF), BF16),
             pltpu.VMEM((LAYERS, NY, 2, HD, HALF), BF16),
             pltpu.VMEM((2, NH, HALF, 128), BF16),
@@ -536,6 +579,8 @@
             dma((LAYERS, NZ)),
             dma((LAYERS, NZ)),
             dma((LAYERS, NZ)),
+            dma((LAYERS, NEAR - 1)),
+            dma((LAYERS, NEAR - 1)),
             dma((LAYERS, NY, 2)),
             dma((LAYERS, NY, 2)),
             dma((2, 7)),

time: 69.9 us -> 68.7 us (0.983); the launches traced: 69.1 us -> 68.6 us
  no operation moved by 1% of the time
where the time goes in v4:
time: 68.7 us; the launch traced here: 68.6 us
  Pallas kernels  68 us (99%)
    pallas_call x1, Pallas kernels, per_device(): pl.pallas_call(kernel, out_shape=jax.ShapeDtypeStruct((ROWS, D), BF16), i...  68 us

profile of v4, /device:TPU:65, one launch (start us, length us, event | category | flops | bytes accessed | tf_op | source)
XLA Modules:
  0.0 68.6 jit_solution(11175992507139195560)
XLA Ops:
  0.0 68.0 %shard_map.55 = bf16[32,1024]{1,0:T(8,128)(2,1)S(1)} custom-call(bf16[32,1024]{1,0:T(8,128)(2,1)} %residual.1, f32[2,1024]{1,0:T(2,128)} %in_gain_hbm.1, bf16[2,3,1024,128]{3,2,1,0:T(8,128)(2,1)} %w_in.1, f32[2,128]{1,0:T(2,128)} %out_gain_hbm.1, bf16[2,128,1024]{2,1,0:T(8,128)(2,1)} %w_out.1), custom_call_target="tpu_custom_call" | custom-call | flops 1500000000 | bytes 3000000 | tf_op jit(solution)/shard_map/pallas_call | solution.py:533
  68.0 0.6 copy.7

commit v5 on v4

--- a/solution.py
+++ b/solution.py
@@ -235,13 +235,17 @@
         exchange = {}
         for f in range(2):
             part = pl.ds(f * HALF, HALF)
-            gather_arrive(halves[f], more[f])
             sent.extend(halves[f] + more[f])
             if layer == 0:
+                gather_arrive(halves[f], more[f])
                 wide = rows_buf[f].reshape(HALF, D).astype(F32)
             else:
-                columns = jnp.concatenate([mix_buf[f, n] for n in range(NH)], axis=1)
-                delta = mm(columns, wout_buf[0].reshape(D, D))
+                delta = jnp.zeros((HALF, D), F32)
+                for step, arrival in zip((0,) + FAR, halves[f][:1] + more[f]):
+                    arrival.wait_recv()
+                    chip = (x + NX - step) % NX
+                    columns = jnp.concatenate([mix_buf[f, 2 * chip + c] for c in range(2)], axis=1)
+                    delta += mm(columns, wout_buf[0, pl.ds(2 * chip, 2)].reshape(2 * 128, D))
                 wide = (resid[part, :] + delta).astype(BF16).astype(F32)
             resid[part, :] = wide
             mean_square = jnp.mean(wide * wide, axis=1, keepdims=True)
@@ -315,24 +319,23 @@
                 make_features(wide_k, feat_k, step, (f,))
                 if f == 1:
                     add_state(step)
+        for r in range(NZ):
+            pieces = []
+            for p in range(PAIRS):
+                at = ((r // 2) * PAIRS + p) * 16 + (r % 2) * 8
+                both = jnp.where(low, state[0, pl.ds(at, 8), :], state[1, pl.ds(at, 8), :])
+                pieces.append(both * factor(p))
+            state_out[layer, r] = jnp.concatenate(pieces, axis=0).astype(BF16)
         if layer == 0:
             hear_round(2)
-        for step in ZFAR + (0,):
-            r = (z + step) % NZ
-            first = (r // 2) * (PAIRS * 16) + (r % 2) * 8
-            pieces = []
-            for p in range(PAIRS):
-                rows = pl.ds(pl.multiple_of(first + p * 16, 8), 8)
-                pieces.append(jnp.where(low, state[0, rows, :], state[1, rows, :]) * factor(p))
-            state_out[layer, r] = jnp.concatenate(pieces, axis=0).astype(BF16)
-            if step:
-                exchange["s", step] = send(
-                    state_out.at[layer, r],
-                    state_in.at[layer, z],
-                    state_send.at[layer, step],
-                    state_recv.at[layer, step],
-                    (at_z(step), head),
-                )
+        for step in ZFAR:
+            exchange["s", step] = send(
+                state_out.at[layer, (z + step) % NZ],
+                state_in.at[layer, z],
+                state_send.at[layer, step],
+                state_recv.at[layer, step],
+                (at_z(step), head),
+            )
         state_in[layer, z] = state_out[layer, z]
 
         def early_copy(reach):

time: 68.7 us -> 68.4 us (level)
  no operation moved by 1% of the time
where the time goes in v5:
time: 68.4 us; the launch traced here: 68.3 us
  Pallas kernels  67.7 us (99%)
    pallas_call x1, Pallas kernels, per_device(): pl.pallas_call(kernel, out_shape=jax.ShapeDtypeStruct((ROWS, D), BF16), i...  67.7 us

profile of v5, /device:TPU:65, one launch (start us, length us, event | category | flops | bytes accessed | tf_op | source)
XLA Modules:
  0.0 68.3 jit_solution(6088884187130809106)
XLA Ops:
  0.0 67.7 %shard_map.55 = bf16[32,1024]{1,0:T(8,128)(2,1)S(1)} custom-call(bf16[32,1024]{1,0:T(8,128)(2,1)} %residual.1, f32[2,1024]{1,0:T(2,128)} %in_gain_hbm.1, bf16[2,3,1024,128]{3,2,1,0:T(8,128)(2,1)} %w_in.1, f32[2,128]{1,0:T(2,128)} %out_gain_hbm.1, bf16[2,128,1024]{2,1,0:T(8,128)(2,1)} %w_out.1), custom_call_target="tpu_custom_call" | custom-call | flops 1500000000 | bytes 3000000 | tf_op jit(solution)/shard_map/pallas_call | solution.py:536
  67.7 0.6 copy.7
